TPU v7x, 128 devices: a whole 4x4x4 slice. The times are simulated.
128 devices in a mesh: wide: 16 (over x, y_lo, core), narrow: 8 (over y_hi, z).
Axes of the slice: x: 4, y: 4 (y_hi: 2, y_lo: 2; y = y_hi * 2 + y_lo), z: 4, core: 2. Of those that a mesh axis runs over, the one named last changes fastest.
Arguments:
- picture_embedding_matrix: bfloat16 [131072, 1152], P(('wide', 'narrow')), may hold values from -0.19921875 to 0.19921875
- caption_embedding_matrix: bfloat16 [131072, 1152], P(('wide', 'narrow')), may hold values from -0.19921875 to 0.19921875
- inverse_softness: float32 [1], replicated, may hold values from 3 to 16
- additive_shift_term: float32 [1], replicated, may hold values from -3 to 0
Outputs:
- image_grad: float32 [131072, 1152], P(('wide', 'narrow'))
- text_grad: float32 [131072, 1152], P(('wide', 'narrow'))
All inputs are finite; a program needn't handle non-finite values.
Results may differ from a plain program's by a relative error of at most 0.0046.
Values may be sent and summed in bfloat16 or wider, within the bound.
No kernel may reach another device: no remote copies, remote signals or barrier semaphores. Data moves between devices by JAX's collectives and lax.ppermute only.
A program may use at most 128 MiB of HBM per device.

v0:
```python
import jax
import jax.numpy as jnp
from jax import lax
from jax.sharding import PartitionSpec as P

BAND = 4


def passed_along(block, axis, distance):
    devices = range(lax.axis_size(axis))
    route = [((i - distance) % len(devices), i) for i in devices]
    return lax.ppermute(block, axis, route)


def rescale_lines_to_length_one(raw):
    widened_float32 = raw.astype(jnp.float32)
    inverse = lax.rsqrt(jnp.sum(widened_float32 * widened_float32, axis=-1, keepdims=True) + 1e-06)
    return (widened_float32 * inverse, inverse)


def pair_weights(logits, positive):
    signs = 2.0 * positive - 1.0
    return (-signs * jax.nn.sigmoid(-signs * logits)).astype(jnp.bfloat16)


def back_normal(unit, inverse, direction):
    inner = jnp.sum(unit * direction, axis=-1, keepdims=True)
    return inverse * (direction - unit * inner)


def block_weights(left, right, positive, similarity_multiplier, bias_value):
    logits = (
        similarity_multiplier * jnp.dot(left, right.T, preferred_element_type=jnp.float32)
        + bias_value
    )
    return pair_weights(logits, positive)


def block_terms(left, right, positive, similarity_multiplier, bias_value):
    pair_label_weights = block_weights(left, right, positive, similarity_multiplier, bias_value)
    to_image = similarity_multiplier * jnp.dot(
        pair_label_weights, right, preferred_element_type=jnp.float32
    )
    to_text = similarity_multiplier * jnp.dot(
        pair_label_weights.T, left, preferred_element_type=jnp.float32
    )
    return (to_image, to_text)


def body(picture_embedding_matrix, caption_embedding_matrix, inverse_softness, additive_shift_term):
    local_line_count = picture_embedding_matrix.shape[0]
    image_unit, image_inv = rescale_lines_to_length_one(picture_embedding_matrix)
    text_unit, text_inv = rescale_lines_to_length_one(caption_embedding_matrix)
    image_low = image_unit.astype(jnp.bfloat16)
    text_low = text_unit.astype(jnp.bfloat16)
    similarity_multiplier = inverse_softness[0]
    bias_value = additive_shift_term[0]
    rows_idx = jnp.arange(local_line_count, dtype=jnp.int32)
    diagonal = (rows_idx[:, None] == rows_idx[None, :]).astype(jnp.float32)
    off_band = jnp.zeros_like(diagonal)
    image_dir, text_dir = block_terms(
        image_low, text_low, diagonal, similarity_multiplier, bias_value
    )
    visiting_block = text_low
    carried = None
    for offset in range(1, BAND):
        visiting_block = passed_along(visiting_block, ("wide", "narrow"), 1)
        to_image, to_text = block_terms(
            image_low, visiting_block, off_band, similarity_multiplier, bias_value
        )
        image_dir = image_dir + to_image
        if carried is None:
            carried = to_text
        else:
            carried = passed_along(carried, ("wide", "narrow"), 1) + to_text
    text_dir = text_dir + passed_along(carried, ("wide", "narrow"), 1 - BAND)
    image_grad = back_normal(image_unit, image_inv, image_dir)
    text_grad = back_normal(text_unit, text_inv, text_dir)
    return (image_grad, text_grad)


def solution(mesh):
    return jax.shard_map(
        body,
        mesh=mesh,
        in_specs=(P(("wide", "narrow"), None), P(("wide", "narrow"), None), P(), P()),
        out_specs=(P(("wide", "narrow"), None), P(("wide", "narrow"), None)),
        check_vma=False,
    )
```

profile of v0, /device:TPU:6, one launch (start us, length us, event | category | flops | bytes accessed | tf_op | source)
XLA Modules:
  0.0 509.6 jit_solution(6994647526952714061)
XLA Ops:
  0.6 0.0 copy-start.1
  0.6 2.3 fusion.13
  3.0 2.1 fusion.2
  5.1 2.0 collective-permute-start
  8.4 0.0 copy-done.1
  8.4 0.5 fusion.9
  9.0 53.5 %collective-permute-done = bf16[1024,1152]{1,0:T(8,128)(2,1)S(1)} collective-permute-done((bf16[1024,1152]{1,0:T(8,128)(2,1)S(1)}, bf16[1024,1152]{1,0:T(8,128)(2,1)S(1)}, u32[]{:S(2)}, u32[]{:S(2)}) %collective-permute-start) | collective-permute-done | bytes 2359328 | tf_op jit(solution)/shard_map/ppermute | solution.py:12
  62.4 0.0 copy-start.4
  62.4 3.7 divide_convert_fusion.2
  66.2 0.0 copy-start.8
  66.2 3.1 convolution_multiply_fusion.2
  69.3 0.0 copy-done.8
  69.3 0.1 collective-permute-start.3
  69.4 0.0 copy-done.4
  69.4 0.1 collective-permute-start.1
  69.5 158.6 %collective-permute-done.1 = bf16[1024,1152]{1,0:T(8,128)(2,1)S(1)} collective-permute-done((bf16[1024,1152]{1,0:T(8,128)(2,1)S(1)}, bf16[1024,1152]{1,0:T(8,128)(2,1)S(1)}, u32[]{:S(2)}, u32[]{:S(2)}) %collective-permute-start.1) | collective-permute-done | bytes 2359328 | tf_op jit(solution)/shard_map/ppermute | solution.py:12
  228.1 3.7 divide_convert_fusion.1
  231.8 0.0 copy-start.6
  231.8 0.0 collective-permute-done.3
  231.8 3.0 fusion.14
  234.9 0.0 copy-done.6
  234.9 0.3 collective-permute-start.4
  235.2 0.1 collective-permute-start.2
  235.2 158.4 %collective-permute-done.2 = bf16[1024,1152]{1,0:T(8,128)(2,1)S(1)} collective-permute-done((bf16[1024,1152]{1,0:T(8,128)(2,1)S(1)}, bf16[1024,1152]{1,0:T(8,128)(2,1)S(1)}, u32[]{:S(2)}, u32[]{:S(2)}) %collective-permute-start.2) | collective-permute-done | bytes 2359328 | tf_op jit(solution)/shard_map/ppermute | solution.py:12
  393.6 0.0 copy-start.2
  393.6 3.7 divide_convert_fusion
  397.3 0.0 copy-done.2
  397.4 0.0 copy-start.3
  397.4 3.1 convolution_multiply_fusion
  400.5 0.0 collective-permute-done.4
  400.5 0.5 add.80
  401.0 0.0 copy-done.3
  401.0 0.3 collective-permute-start.5
  401.3 4.5 multiply_convert_fusion
  405.8 2.9 fusion.23
  408.7 0.0 copy-start.5
  408.7 0.0 copy-start.9
  408.8 3.1 convolution_multiply_fusion.3
  411.9 0.0 copy-done.5
  411.9 0.0 copy-done.9
  411.9 0.0 copy-start.7
  411.9 4.5 fusion.24
  416.5 0.0 copy-done.7
  416.5 4.5 fusion.25
  420.9 8.7 %fusion.6 = (f32[1024]{0:T(1024)S(1)}, f32[1024,1152]{1,0:T(8,128)S(1)}) fusion(bf16[1024,1152]{1,0:T(8,128)(2,1)S(1)} %copy-done.1, f32[1024]{0:T(1024)S(1)} %add_rsqrt_fusion.1, f32[]{:T(128)} %bitcast.18, bf16[1024,1024]{1,0:T(8,128)(2,1)} %copy-done.3, bf16[1024,1152]{1,0:T(8,128)(2,1)} %copy-done.2, f32[1024,1152]{1,0:T(8,128)} %fusion.25, ...), kind=kOutput, calls=%fused_computation.14 | convolution fusion | flops 2425355264 | bytes 25698308 | tf_op jit(solution)/shard_map/dot_general | solution.py:41
  429.6 0.0 copy-start
  429.6 3.1 fusion.8
  432.7 72.9 %collective-permute-done.5 = f32[1024,1152]{1,0:T(8,128)S(1)} collective-permute-done((f32[1024,1152]{1,0:T(8,128)S(1)}, f32[1024,1152]{1,0:T(8,128)S(1)}, u32[]{:S(2)}, u32[]{:S(2)}) %collective-permute-start.5) | collective-permute-done | bytes 4718624 | tf_op jit(solution)/shard_map/ppermute | solution.py:12
  505.6 0.0 copy-done
  505.6 0.9 fusion.10
  506.6 3.1 fusion.12
  (2 shorter events, 0.0 us)
Async XLA Ops:
  0.6 7.8 %copy-start.1 = (bf16[1024,1152]{1,0:T(8,128)(2,1)S(1)}, bf16[1024,1152]{1,0:T(8,128)(2,1)}, u32[]{:S(2)}) copy-start(bf16[1024,1152]{1,0:T(8,128)(2,1)} %param.4) | copy-start | bytes 7077892
  5.1 57.3 %collective-permute-start = (bf16[1024,1152]{1,0:T(8,128)(2,1)S(1)}, bf16[1024,1152]{1,0:T(8,128)(2,1)S(1)}, u32[]{:S(2)}, u32[]{:S(2)}) collective-permute-start(bf16[1024,1152]{1,0:T(8,128)(2,1)S(1)} %fusion.2), channel_id=1, source_target_pairs={{127,0},{0,1},{1,2},{2,3},{3,4},{4,5},{5,6},{6,7},{7,8},{8,9},{9,1... | collective-permute-start | bytes 7077896 | tf_op jit(solution)/shard_map/ppermute | solution.py:12
  62.4 6.9 %copy-start.4 = (bf16[1024,1152]{1,0:T(8,128)(2,1)}, bf16[1024,1152]{1,0:T(8,128)(2,1)S(1)}, u32[]{:S(2)}) copy-start(bf16[1024,1152]{1,0:T(8,128)(2,1)S(1)} %collective-permute-done) | copy-start | bytes 7077892
  66.2 3.1 copy-start.8
  69.3 162.5 %collective-permute-start.3 = (f32[1024,1152]{1,0:T(8,128)S(1)}, f32[1024,1152]{1,0:T(8,128)S(1)}, u32[]{:S(2)}, u32[]{:S(2)}) collective-permute-start(f32[1024,1152]{1,0:T(8,128)S(1)} %convolution_multiply_fusion.2), channel_id=1, source_target_pairs={{127,0},{0,1},{1,2},{2,3},{3,4},{4,5},{5,6},{6,7},{7,8},{8,9},{9,1... | collective-permute-start | bytes 14155784 | tf_op jit(solution)/shard_map/ppermute | solution.py:12
  69.4 158.7 %collective-permute-start.1 = (bf16[1024,1152]{1,0:T(8,128)(2,1)S(1)}, bf16[1024,1152]{1,0:T(8,128)(2,1)S(1)}, u32[]{:S(2)}, u32[]{:S(2)}) collective-permute-start(bf16[1024,1152]{1,0:T(8,128)(2,1)S(1)} %collective-permute-done), channel_id=1, source_target_pairs={{127,0},{0,1},{1,2},{2,3},{3,4},{4,5},{5,6},{6,7},{7,8},{8,9},{9,1... | collective-permute-start | bytes 7077896 | tf_op jit(solution)/shard_map/ppermute | solution.py:12
  231.8 3.0 copy-start.6
  234.9 165.6 %collective-permute-start.4 = (f32[1024,1152]{1,0:T(8,128)S(1)}, f32[1024,1152]{1,0:T(8,128)S(1)}, u32[]{:S(2)}, u32[]{:S(2)}) collective-permute-start(f32[1024,1152]{1,0:T(8,128)S(1)} %fusion.14), channel_id=1, source_target_pairs={{127,0},{0,1},{1,2},{2,3},{3,4},{4,5},{5,6},{6,7},{7,8},{8,9},{9,1... | collective-permute-start | bytes 14155784 | tf_op jit(solution)/shard_map/ppermute | solution.py:12
  235.2 158.4 %collective-permute-start.2 = (bf16[1024,1152]{1,0:T(8,128)(2,1)S(1)}, bf16[1024,1152]{1,0:T(8,128)(2,1)S(1)}, u32[]{:S(2)}, u32[]{:S(2)}) collective-permute-start(bf16[1024,1152]{1,0:T(8,128)(2,1)S(1)} %collective-permute-done.1), channel_id=1, source_target_pairs={{127,0},{0,1},{1,2},{2,3},{3,4},{4,5},{5,6},{6,7},{7,8},{8,9},{9,1... | collective-permute-start | bytes 7077896 | tf_op jit(solution)/shard_map/ppermute | solution.py:12
  393.6 3.7 copy-start.2
  397.4 3.6 copy-start.3
  401.0 104.6 %collective-permute-start.5 = (f32[1024,1152]{1,0:T(8,128)S(1)}, f32[1024,1152]{1,0:T(8,128)S(1)}, u32[]{:S(2)}, u32[]{:S(2)}) collective-permute-start(f32[1024,1152]{1,0:T(8,128)S(1)} %add.80), channel_id=1, source_target_pairs={{3,0},{4,1},{5,2},{6,3},{7,4},{8,5},{9,6},{10,7},{11,8},{12,9},{13... | collective-permute-start | bytes 14155784 | tf_op jit(solution)/shard_map/ppermute | solution.py:12
  408.7 3.2 copy-start.5
  408.7 3.2 copy-start.9
  411.9 4.5 copy-start.7
  429.6 76.0 %copy-start = (bf16[1024,1152]{1,0:T(8,128)(2,1)S(1)}, bf16[1024,1152]{1,0:T(8,128)(2,1)}, u32[]{:S(2)}) copy-start(bf16[1024,1152]{1,0:T(8,128)(2,1)} %param.5) | copy-start | bytes 7077892
where the time goes:
time: 510 us
  waiting for transfers between devices  443 us (87%)
  matrix products  48.7 us (10%)
  other arithmetic  12.5 us (2%)
    ppermute x6, waiting for transfers between devices, passed_along(): return lax.ppermute(block, axis, route)  443 us
    dot_general x4, matrix products, block_terms(): jnp.dot(pair_label_weights, right, preferred_element_type=jnp.float32)  20.6 us
    dot_general x4, matrix products, block_weights(): jnp.dot(left, right.T, preferred_element_type=jnp.float32)  15.7 us
    dot_general x4, matrix products, block_terms(): jnp.dot(pair_label_weights.T, left, preferred_element_type=jnp.float32)  12.4 us
  transfers between devices with their start and end apart: 6, of which 4 were waited for; matrix products, arithmetic and copies ran while one was open for 8% of the time, Pallas kernels for 0%

commit v1 on v0

v1 whole, which is shorter than its diff:
```python
import functools

import jax
import jax.numpy as jnp
from jax import lax
from jax.experimental import pallas as pl
from jax.experimental.pallas import tpu as pltpu
from jax.sharding import PartitionSpec as P

AXES = ("wide", "narrow")
RING = 4
VMEM_BYTES = 48 * 1024 * 1024


def ring_route(step, count):
    return [(d, d - d % RING + (d + step) % RING) for d in range(count)]


def line_route(step, count):
    return [(d, (d + step) % count) for d in range(count)]


def send(block, route):
    return lax.ppermute(block, AXES, route)


def unit_rows(raw):
    wide = raw.astype(jnp.float32)
    inverse = lax.rsqrt(jnp.sum(wide * wide, axis=-1, keepdims=True) + 1e-06)
    return wide * inverse, inverse


def unit_kernel(raw_ref, *refs):
    unit, _ = unit_rows(raw_ref[...])
    refs[-1][0] = unit.astype(jnp.bfloat16)


def unit_images(raw, slot, held=None):
    rows, width = raw.shape
    tile = rows // 4
    aliased = [] if held is None else [held]
    return pl.pallas_call(
        unit_kernel,
        grid=(4,),
        out_shape=jax.ShapeDtypeStruct((2, rows, width), jnp.bfloat16),
        in_specs=[pl.BlockSpec((tile, width), lambda i: (i, 0))]
        + [pl.BlockSpec(memory_space=pl.ANY)] * len(aliased),
        out_specs=pl.BlockSpec((1, tile, width), lambda i: (slot, i, 0)),
        input_output_aliases={} if held is None else {1: 0},
        cost_estimate=pl.CostEstimate(
            flops=4 * rows * width, bytes_accessed=4 * rows * width, transcendentals=0
        ),
    )(raw, *aliased)


def dot(left, right, contract):
    return lax.dot_general(
        left, right, (contract, ((), ())), preferred_element_type=jnp.float32
    )


def pair_kernel(own, tile, slot_ref, scalars_ref, text_ref, images_ref, *refs):
    if own:
        sum_in = None
        partial_ref, sum_ref, images, low, weights, total, sems = refs
    else:
        sum_in, partial_ref, sum_ref, images, low, weights, total, sems = refs
    rows = text_ref.shape[0]
    slot = slot_ref[0]
    scale = scalars_ref[0]
    bias = scalars_ref[1]
    load_images = pltpu.make_async_copy(images_ref.at[slot], images, sems.at[0])
    load_images.start()
    if own:
        zero_tile = total.at[pl.ds(0, tile)]
        total[pl.ds(0, tile), :] = jnp.zeros((tile, total.shape[1]), jnp.float32)
        clears = [
            pltpu.make_async_copy(
                zero_tile, sum_ref.at[1, pl.ds(i * tile, tile)], sems.at[1 + i]
            )
            for i in range(total.shape[0] // tile)
        ]
        for clear in clears:
            clear.start()
    else:
        load_sum = pltpu.make_async_copy(sum_in.at[slot], total, sems.at[1])
        load_sum.start()
    unit, _ = unit_rows(text_ref[...])
    low[...] = unit.astype(jnp.bfloat16)
    load_images.wait()

    @pl.loop(0, rows // tile)
    def _(i):
        here = pl.ds(pl.multiple_of(i * tile, tile), tile)
        logits = scale * dot(low[here, :], images[...], ((1,), (1,))) + bias
        if own:
            row = i * tile + lax.broadcasted_iota(jnp.int32, logits.shape, 0)
            column = lax.broadcasted_iota(jnp.int32, logits.shape, 1)
            sign = jnp.where(row == column, -1.0, 1.0)
            weight = sign / (1.0 + jnp.exp(-(sign * logits)))
        else:
            weight = 1.0 / (1.0 + jnp.exp(-logits))
        weights[here, :] = weight.astype(jnp.bfloat16)
        product = dot(weights[here, :], images[...], ((1,), (0,)))
        partial_ref[here, :] = (scale * product).astype(partial_ref.dtype)

    if own:
        for clear in clears:
            clear.wait()
    else:
        load_sum.wait()

    @pl.loop(0, total.shape[0] // tile)
    def _(i):
        here = pl.ds(pl.multiple_of(i * tile, tile), tile)
        product = scale * dot(weights[:, here], low[...], ((0,), (0,)))
        total[here, :] = product if own else total[here, :] + product

    store_sum = pltpu.make_async_copy(total, sum_ref.at[slot], sems.at[0])
    store_sum.start()
    store_sum.wait()


def pair(slot, scalars, text, images, sums, partial_dtype, tile=256):
    own = sums is None
    rows, width = text.shape
    image_rows = images.shape[1]
    any_spec = pl.BlockSpec(memory_space=pl.ANY)
    smem = pl.BlockSpec(memory_space=pltpu.SMEM)
    vmem = pl.BlockSpec(memory_space=pltpu.VMEM)
    return pl.pallas_call(
        functools.partial(pair_kernel, own, tile),
        out_shape=(
            jax.ShapeDtypeStruct((rows, width), partial_dtype),
            jax.ShapeDtypeStruct((2, image_rows, width), jnp.float32),
        ),
        in_specs=[smem, smem, vmem, any_spec] + ([] if own else [any_spec]),
        out_specs=(vmem, any_spec),
        input_output_aliases={} if own else {4: 1},
        scratch_shapes=[
            pltpu.VMEM((image_rows, width), jnp.bfloat16),
            pltpu.VMEM((rows, width), jnp.bfloat16),
            pltpu.VMEM((rows, image_rows), jnp.bfloat16),
            pltpu.VMEM((image_rows, width), jnp.float32),
            pltpu.SemaphoreType.DMA((1 + image_rows // tile,)),
        ],
        compiler_params=pltpu.CompilerParams(vmem_limit_bytes=VMEM_BYTES),
        cost_estimate=pl.CostEstimate(
            flops=6 * rows * image_rows * width,
            bytes_accessed=8 * image_rows * width + 4 * rows * width,
            transcendentals=rows * image_rows,
        ),
    )(slot, scalars, text, images, *([] if own else [sums]))


def finish_kernel(raw_ref, base_ref, *refs):
    grad_ref = refs[-1]
    unit, inverse = unit_rows(raw_ref[...])
    direction = base_ref[...].reshape(unit.shape)
    for part in refs[:-1]:
        direction = direction + part[...].astype(jnp.float32)
    inner = jnp.sum(unit * direction, axis=-1, keepdims=True)
    grad_ref[...] = inverse * (direction - unit * inner)


def finish(raw, base, parts, tile=128):
    rows, width = raw.shape
    flat = pl.BlockSpec((tile, width), lambda i: (i, 0))
    base_spec = flat if base.ndim == 2 else pl.BlockSpec((1, tile, width), lambda i: (0, i, 0))
    return pl.pallas_call(
        finish_kernel,
        grid=(rows // tile,),
        out_shape=jax.ShapeDtypeStruct((rows, width), jnp.float32),
        in_specs=[flat, base_spec] + [flat] * len(parts),
        out_specs=flat,
        cost_estimate=pl.CostEstimate(
            flops=8 * rows * width, bytes_accessed=12 * rows * width, transcendentals=0
        ),
    )(raw, base, *parts)


def body(images_raw, texts_raw, inverse_softness, additive_shift_term):
    count = lax.axis_size("wide") * lax.axis_size("narrow")
    z = lax.axis_index("narrow") % RING
    scalars = jnp.concatenate([inverse_softness, additive_shift_term])
    slots = [jnp.zeros((1,), jnp.int32)] + [
        jnp.where(z < RING - t, 1, 0).astype(jnp.int32).reshape(1) for t in (1, 2, 3)
    ]
    up, down = ring_route(1, count), ring_route(-1, count)
    half = texts_raw.shape[0] // 2
    own_a, own_b = texts_raw[:half], texts_raw[half:]

    images_next_raw = send(images_raw, line_route(-RING, count))
    left_a = send(own_a, up)
    right_b = send(own_b, down)

    images = unit_images(images_raw, 0)
    text_own, sums = pair(slots[0], scalars, texts_raw, images, None, jnp.float32)

    left_b = send(own_b, up)
    right_a = send(own_a, down)
    far_a = send(left_a, up)
    far_b = send(right_b, down)

    images = unit_images(images_next_raw, 1, images)
    step = lambda t, text, total, kind: pair(slots[t], scalars, text, images, total, kind)
    part_left_a, sums = step(3, left_a, sums, jnp.bfloat16)
    part_right_b, sums = step(1, right_b, sums, jnp.bfloat16)
    from_right_a = send(part_left_a, down)
    from_left_b = send(part_right_b, up)
    part_far_a, sums = step(2, far_a, sums, jnp.bfloat16)
    part_far_b, sums = step(2, far_b, sums, jnp.bfloat16)
    far_for_right_a = send(part_far_a, up)
    far_for_left_b = send(part_far_b, down)
    part_right_a, sums = step(1, right_a, sums, jnp.float32)
    part_left_b, sums = step(3, left_b, sums, jnp.float32)
    images_back = send(sums[1].astype(jnp.bfloat16), line_route(RING, count))
    from_left_a = send(
        (part_right_a + far_for_right_a.astype(jnp.float32)).astype(jnp.bfloat16), up
    )
    from_right_b = send(
        (part_left_b + far_for_left_b.astype(jnp.float32)).astype(jnp.bfloat16), down
    )
    image_grad = finish(images_raw, sums, [images_back])
    text_grad = finish(
        texts_raw,
        text_own,
        [
            jnp.concatenate([from_right_a, from_left_b]),
            jnp.concatenate([from_left_a, from_right_b]),
        ],
    )
    return image_grad, text_grad


def solution(mesh):
    spec = P(AXES, None)
    return jax.shard_map(
        body,
        mesh=mesh,
        in_specs=(spec, spec, P(), P()),
        out_specs=(spec, spec),
        check_vma=False,
    )
```

time: 510 us -> 210 us (0.41)
  waiting for transfers between devices: 443 us -> 65 us
  Pallas kernels: 0 us -> 106 us
  matrix products: 48.7 us -> 0 us
  starting transfers between devices: 2.81 us -> 22.2 us
  local copies, waits for them, and re-layouts: 0.05 us -> 8.6 us
  other arithmetic: 12.5 us -> 5.08 us
    ppermute x6 -> x14, waiting for transfers between devices: 443 us -> 65 us  [send(): return lax.ppermute(block, AXES, route)]
    pallas_call x0 -> x11, Pallas kernels: none -> 106 us  [the longest x7 80.2 us: pair(): pl.pallas_call(functools.partial(pair_kernel, own, tile), out_shape=(jax....]
    dot_general x12 -> x0, matrix products: 48.7 us -> none  [the longest x4 20.6 us: block_terms(): jnp.dot(pair_label_weights, right, preferred_element_type=jnp.float32)]
    ppermute x6 -> x14, starting transfers between devices: 2.81 us -> 22.2 us  [send(): return lax.ppermute(block, AXES, route)]
    mul x2 -> x0, other arithmetic: 6.13 us -> none  [back_normal(): return inverse * (direction - unit * inner)]
  transfers between devices with their start and end apart: 6 -> 14, of which waited for: 4 -> 6; matrix products, arithmetic and copies ran while one was open for 8% -> 6% of each run, Pallas kernels for 0% -> 47%
where the time goes in v1:
time: 210 us; the launch traced here: 209 us
  Pallas kernels  106 us (50%)
  waiting for transfers between devices  65 us (31%)
  starting transfers between devices  22.2 us (11%)
  local copies, waits for them, and re-layouts  8.6 us (4%)
  other arithmetic  5.08 us (2%)
    pallas_call x7, Pallas kernels, pair(): pl.pallas_call(functools.partial(pair_kernel, own, tile), out_shape=(jax....  80.2 us
    ppermute x14, waiting for transfers between devices, send(): return lax.ppermute(block, AXES, route)  65 us
    ppermute x14, starting transfers between devices, send(): return lax.ppermute(block, AXES, route)  22.2 us
    pallas_call x2, Pallas kernels, finish(): pl.pallas_call(finish_kernel, grid=(rows // tile,), out_shape=jax.ShapeDt...  17.7 us
    pallas_call x2, Pallas kernels, unit_images(): pl.pallas_call(unit_kernel, grid=(4,), out_shape=jax.ShapeDtypeStruct((2,...  8.58 us
  transfers between devices with their start and end apart: 14, of which 6 were waited for; matrix products, arithmetic and copies ran while one was open for 6% of the time, Pallas kernels for 47%

profile of v1, /device:TPU:6, one launch (start us, length us, event | category | flops | bytes accessed | tf_op | source)
XLA Modules:
  0.0 209.5 jit_solution(9298802870719699643)
XLA Ops:
  0.6 2.8 %collective-permute-start.1 = (bf16[1024,1152]{1,0:T(8,128)(2,1)}, bf16[1024,1152]{1,0:T(8,128)(2,1)}, u32[]{:S(2)}, u32[]{:S(2)}) collective-permute-start(bf16[1024,1152]{1,0:T(8,128)(2,1)} %raw_ref.4), channel_id=1, source_target_pairs={{0,124},{1,125},{2,126},{3,127},{4,0},{5,1},{6,2},{7,3},{8,4},{9,5... | collective-permute-start | bytes 7077896 | tf_op jit(solution)/shard_map/ppermute | solution.py:24
  3.4 3.3 %fusion.1 = (bf16[512,1152]{1,0:T(8,128)(2,1)}, bf16[512,1152]{1,0:T(8,128)(2,1)}) fusion(bf16[1024,1152]{1,0:T(8,128)(2,1)} %raw_ref.5), kind=kLoop, calls=%fused_computation.7 | loop fusion | bytes 4718592 | tf_op jit(solution)/shard_map/slice | solution.py:191
  6.7 1.9 collective-permute-start.5
  8.6 2.1 %collective-permute-start.3 = (bf16[512,1152]{1,0:T(8,128)(2,1)}, bf16[512,1152]{1,0:T(8,128)(2,1)}, u32[]{:S(2)}, u32[]{:S(2)}) collective-permute-start(bf16[512,1152]{1,0:T(8,128)(2,1)} %get-tuple-element.31), channel_id=1, source_target_pairs={{0,3},{1,0},{2,1},{3,2},{4,7},{5,4},{6,5},{7,6},{8,11},{9,8},{10,9... | collective-permute-start | bytes 3538952 | tf_op jit(solution)/shard_map/ppermute | solution.py:24
  10.7 2.0 collective-permute-start.2
  12.7 0.0 collective-permute-start
  14.0 0.0 copy-start
  14.1 4.4 %shard_map.59.refs_0_.images_ref = bf16[2,1024,1152]{2,1,0:T(8,128)(2,1)} custom-call(bf16[1024,1152]{1,0:T(8,128)(2,1)} %raw_ref.4), custom_call_target="tpu_custom_call" | custom-call | flops 4718592 | bytes 4718592 | tf_op jit(solution)/shard_map/pallas_call | solution.py:42
  18.4 0.1 pad_maximum_fusion.2.scalars_ref
  18.5 19.4 %collective-permute-done.5.text_ref = bf16[512,1152]{1,0:T(8,128)(2,1)} collective-permute-done((bf16[512,1152]{1,0:T(8,128)(2,1)}, bf16[512,1152]{1,0:T(8,128)(2,1)}, u32[]{:S(2)}, u32[]{:S(2)}) %collective-permute-start.5) | collective-permute-done | bytes 1179680 | tf_op jit(solution)/shard_map/ppermute | solution.py:24
  37.9 0.0 collective-permute-start.6
  37.9 0.0 collective-permute-done.3.text_ref
  37.9 3.2 %collective-permute-start.4 = (bf16[512,1152]{1,0:T(8,128)(2,1)}, bf16[512,1152]{1,0:T(8,128)(2,1)}, u32[]{:S(2)}, u32[]{:S(2)}) collective-permute-start(bf16[512,1152]{1,0:T(8,128)(2,1)} %collective-permute-done.3.text_ref), channel_id=1, source_target_pairs={{0,3},{1,0},{2,1},{3,2},{4,7},{5,4},{6,5},{7,6},{8,11},{9,8},{10,9... | collective-permute-start | bytes 3538952 | tf_op jit(solution)/shard_map/ppermute | solution.py:24
  41.1 0.0 copy-done
  41.1 17.2 %shard_map.61 = (f32[1024,1152]{1,0:T(8,128)}, f32[2,1024,1152]{2,1,0:T(8,128)}) custom-call(s32[1]{0:T(128)} %constant.24.clone.1.slot_ref, f32[2]{0:T(128)S(1)} %pad_maximum_fusion.2.scalars_ref, bf16[1024,1152]{1,0:T(8,128)(2,1)S(1)} %copy-done, bf16[2,1024,1152]{2,1,0:T(8,128)(2,1)} %shard_map.59.refs_0_.images_ref), custom_call_target="tpu_custom_call" | custom-call | flops 7247757312 | bytes 14155776 | tf_op jit(solution)/shard_map/pallas_call | solution.py:131
  58.4 0.0 collective-permute-done.1.raw_ref
  58.4 4.2 %shard_map.60.images_ref = bf16[2,1024,1152]{2,1,0:T(8,128)(2,1)} custom-call(bf16[1024,1152]{1,0:T(8,128)(2,1)} %collective-permute-done.1.raw_ref, bf16[2,1024,1152]{2,1,0:T(8,128)(2,1)} %shard_map.59.refs_0_.images_ref), custom_call_target="tpu_custom_call", output_to_operand_aliasing={{}: (1, {})} | custom-call | flops 4718592 | bytes 4718592 | tf_op jit(solution)/shard_map/pallas_call | solution.py:42
  62.6 10.6 %shard_map.62 = (bf16[512,1152]{1,0:T(8,128)(2,1)S(1)}, f32[2,1024,1152]{2,1,0:T(8,128)}) custom-call(s32[1]{0:T(128)} %bitcast.slot_ref, f32[2]{0:T(128)S(1)} %pad_maximum_fusion.2.scalars_ref, bf16[512,1152]{1,0:T(8,128)(2,1)} %collective-permute-done.5.text_ref, bf16[2,1024,1152]{2,1,0:T(8,128)(2,1)} %shard_map.60.images_ref, ...), custom_call_target="tpu_custom_call", output_to_operand_aliasing={{1}: (4, {})} | custom-call | flops 3623878656 | bytes 11796480 | tf_op jit(solution)/shard_map/pallas_call | solution.py:131
  73.2 10.6 %shard_map.63 = (bf16[512,1152]{1,0:T(8,128)(2,1)S(1)}, f32[2,1024,1152]{2,1,0:T(8,128)}) custom-call(s32[1]{0:T(128)} %bitcast.1.slot_ref, f32[2]{0:T(128)S(1)} %pad_maximum_fusion.2.scalars_ref, bf16[512,1152]{1,0:T(8,128)(2,1)} %collective-permute-done.3.text_ref, bf16[2,1024,1152]{2,1,0:T(8,128)(2,1)} %shard_map.60.images_ref, ...), custom_call_target="tpu_custom_call", output_to_operand_aliasing={{1}: (4, {})} | custom-call | flops 3623878656 | bytes 11796480 | tf_op jit(solution)/shard_map/pallas_call | solution.py:131
  83.9 4.5 %collective-permute-done.6.text_ref = bf16[512,1152]{1,0:T(8,128)(2,1)} collective-permute-done((bf16[512,1152]{1,0:T(8,128)(2,1)}, bf16[512,1152]{1,0:T(8,128)(2,1)}, u32[]{:S(2)}, u32[]{:S(2)}) %collective-permute-start.6) | collective-permute-done | bytes 1179680 | tf_op jit(solution)/shard_map/ppermute | solution.py:24
  88.3 10.6 %shard_map.64 = (bf16[512,1152]{1,0:T(8,128)(2,1)S(1)}, f32[2,1024,1152]{2,1,0:T(8,128)}) custom-call(s32[1]{0:T(128)} %bitcast.2.slot_ref, f32[2]{0:T(128)S(1)} %pad_maximum_fusion.2.scalars_ref, bf16[512,1152]{1,0:T(8,128)(2,1)} %collective-permute-done.6.text_ref, bf16[2,1024,1152]{2,1,0:T(8,128)(2,1)} %shard_map.60.images_ref, ...), custom_call_target="tpu_custom_call", output_to_operand_aliasing={{1}: (4, {})} | custom-call | flops 3623878656 | bytes 11796480 | tf_op jit(solution)/shard_map/pallas_call | solution.py:131
  98.9 0.1 collective-permute-start.10
  99.0 0.0 collective-permute-done.4.text_ref
  99.0 10.6 %shard_map.65 = (bf16[512,1152]{1,0:T(8,128)(2,1)S(1)}, f32[2,1024,1152]{2,1,0:T(8,128)}) custom-call(s32[1]{0:T(128)} %bitcast.2.slot_ref, f32[2]{0:T(128)S(1)} %pad_maximum_fusion.2.scalars_ref, bf16[512,1152]{1,0:T(8,128)(2,1)} %collective-permute-done.4.text_ref, bf16[2,1024,1152]{2,1,0:T(8,128)(2,1)} %shard_map.60.images_ref, ...), custom_call_target="tpu_custom_call", output_to_operand_aliasing={{1}: (4, {})} | custom-call | flops 3623878656 | bytes 11796480 | tf_op jit(solution)/shard_map/pallas_call | solution.py:131
  109.7 3.5 %collective-permute-start.12 = (bf16[512,1152]{1,0:T(8,128)(2,1)S(1)}, bf16[512,1152]{1,0:T(8,128)(2,1)}, u32[]{:S(2)}, u32[]{:S(2)}) collective-permute-start(bf16[512,1152]{1,0:T(8,128)(2,1)S(1)} %get-tuple-element.29), channel_id=1, source_target_pairs={{0,3},{1,0},{2,1},{3,2},{4,7},{5,4},{6,5},{7,6},{8,11},{9,8},{10,9... | collective-permute-start | bytes 3538952 | tf_op jit(solution)/shard_map/ppermute | solution.py:24
  113.1 0.0 collective-permute-start.9
  113.1 0.0 collective-permute-done.2.text_ref
  113.1 3.2 %collective-permute-start.8 = (bf16[512,1152]{1,0:T(8,128)(2,1)S(1)}, bf16[512,1152]{1,0:T(8,128)(2,1)S(1)}, u32[]{:S(2)}, u32[]{:S(2)}) collective-permute-start(bf16[512,1152]{1,0:T(8,128)(2,1)S(1)} %get-tuple-element.24), channel_id=1, source_target_pairs={{0,3},{1,0},{2,1},{3,2},{4,7},{5,4},{6,5},{7,6},{8,11},{9,8},{10,9... | collective-permute-start | bytes 3538952 | tf_op jit(solution)/shard_map/ppermute | solution.py:24
  116.4 10.6 %shard_map.66 = (f32[512,1152]{1,0:T(8,128)S(1)}, f32[2,1024,1152]{2,1,0:T(8,128)}) custom-call(s32[1]{0:T(128)} %bitcast.1.slot_ref, f32[2]{0:T(128)S(1)} %pad_maximum_fusion.2.scalars_ref, bf16[512,1152]{1,0:T(8,128)(2,1)} %collective-permute-done.2.text_ref, bf16[2,1024,1152]{2,1,0:T(8,128)(2,1)} %shard_map.60.images_ref, ...), custom_call_target="tpu_custom_call", output_to_operand_aliasing={{1}: (4, {})} | custom-call | flops 3623878656 | bytes 11796480 | tf_op jit(solution)/shard_map/pallas_call | solution.py:131
  127.0 0.0 collective-permute-done.text_ref
  127.0 9.9 %shard_map.67 = (f32[512,1152]{1,0:T(8,128)S(1)}, f32[2,1024,1152]{2,1,0:T(8,128)}) custom-call(s32[1]{0:T(128)} %bitcast.slot_ref, f32[2]{0:T(128)S(1)} %pad_maximum_fusion.2.scalars_ref, bf16[512,1152]{1,0:T(8,128)(2,1)S(1)} %collective-permute-done.text_ref, bf16[2,1024,1152]{2,1,0:T(8,128)(2,1)} %shard_map.60.images_ref, ...), custom_call_target="tpu_custom_call", output_to_operand_aliasing={{1}: (4, {})} | custom-call | flops 3623878656 | bytes 11796480 | tf_op jit(solution)/shard_map/pallas_call | solution.py:131
  136.9 4.0 %fusion = bf16[1024,1152]{1,0:T(8,128)(2,1)} fusion(f32[2,1024,1152]{2,1,0:T(8,128)} %get-tuple-element.22.base_ref), kind=kLoop, calls=%fused_computation.1 | loop fusion | bytes 4718592 | tf_op jit(solution)/shard_map/convert_element_type | solution.py:217
  140.8 0.0 collective-permute-start.7
  140.8 0.0 collective-permute-done.10
  140.8 0.3 add_convert_fusion.1
  141.1 0.1 collective-permute-start.11
  141.2 0.0 collective-permute-done.12
  141.2 1.5 add_convert_fusion
  142.8 3.3 %collective-permute-start.13 = (bf16[512,1152]{1,0:T(8,128)(2,1)S(1)}, bf16[512,1152]{1,0:T(8,128)(2,1)S(1)}, u32[]{:S(2)}, u32[]{:S(2)}) collective-permute-start(bf16[512,1152]{1,0:T(8,128)(2,1)S(1)} %add_convert_fusion), channel_id=1, source_target_pairs={{0,3},{1,0},{2,1},{3,2},{4,7},{5,4},{6,5},{7,6},{8,11},{9,8},{10,9... | collective-permute-start | bytes 3538952 | tf_op jit(solution)/shard_map/ppermute | solution.py:24
  146.0 8.3 %collective-permute-done.9 = bf16[512,1152]{1,0:T(8,128)(2,1)S(1)} collective-permute-done((bf16[512,1152]{1,0:T(8,128)(2,1)S(1)}, bf16[512,1152]{1,0:T(8,128)(2,1)S(1)}, u32[]{:S(2)}, u32[]{:S(2)}) %collective-permute-start.9) | collective-permute-done | bytes 1179680 | tf_op jit(solution)/shard_map/ppermute | solution.py:24
  154.3 10.5 %collective-permute-done.8 = bf16[512,1152]{1,0:T(8,128)(2,1)S(1)} collective-permute-done((bf16[512,1152]{1,0:T(8,128)(2,1)S(1)}, bf16[512,1152]{1,0:T(8,128)(2,1)S(1)}, u32[]{:S(2)}, u32[]{:S(2)}) %collective-permute-start.8) | collective-permute-done | bytes 1179680 | tf_op jit(solution)/shard_map/ppermute | solution.py:24
  164.8 1.6 pad_maximum_fusion.refs_0_
  166.4 12.2 %collective-permute-done.11 = bf16[512,1152]{1,0:T(8,128)(2,1)S(1)} collective-permute-done((bf16[512,1152]{1,0:T(8,128)(2,1)S(1)}, bf16[512,1152]{1,0:T(8,128)(2,1)S(1)}, u32[]{:S(2)}, u32[]{:S(2)}) %collective-permute-start.11) | collective-permute-done | bytes 1179680 | tf_op jit(solution)/shard_map/ppermute | solution.py:24
  178.7 10.1 %collective-permute-done.13 = bf16[512,1152]{1,0:T(8,128)(2,1)S(1)} collective-permute-done((bf16[512,1152]{1,0:T(8,128)(2,1)S(1)}, bf16[512,1152]{1,0:T(8,128)(2,1)S(1)}, u32[]{:S(2)}, u32[]{:S(2)}) %collective-permute-start.13) | collective-permute-done | bytes 1179680 | tf_op jit(solution)/shard_map/ppermute | solution.py:24
  188.8 1.6 pad_maximum_fusion.1.refs_1_
  190.4 9.2 %shard_map.69 = f32[1024,1152]{1,0:T(8,128)} custom-call(bf16[1024,1152]{1,0:T(8,128)(2,1)} %raw_ref.5, f32[1024,1152]{1,0:T(8,128)} %get-tuple-element.23.base_ref, bf16[1024,1152]{1,0:T(8,128)(2,1)} %pad_maximum_fusion.refs_0_, bf16[1024,1152]{1,0:T(8,128)(2,1)} %pad_maximum_fusion.1.refs_1_), custom_call_target="tpu_custom_call" | custom-call | flops 9437184 | bytes 14155776 | tf_op jit(solution)/shard_map/pallas_call | solution.py:170
  199.5 0.0 collective-permute-done.7.refs_0_
  199.5 0.0 copy-start.1
  199.5 1.4 copy-done.1
  200.9 8.6 %shard_map.68 = f32[1024,1152]{1,0:T(8,128)} custom-call(bf16[1024,1152]{1,0:T(8,128)(2,1)} %raw_ref.4, f32[2,1024,1152]{2,1,0:T(8,128)} %get-tuple-element.22.base_ref, bf16[1024,1152]{1,0:T(8,128)(2,1)} %copy-done.1), custom_call_target="tpu_custom_call" | custom-call | flops 9437184 | bytes 14155776 | tf_op jit(solution)/shard_map/pallas_call | solution.py:170
Async XLA Ops:
  0.6 57.8 %collective-permute-start.1 = (bf16[1024,1152]{1,0:T(8,128)(2,1)}, bf16[1024,1152]{1,0:T(8,128)(2,1)}, u32[]{:S(2)}, u32[]{:S(2)}) collective-permute-start(bf16[1024,1152]{1,0:T(8,128)(2,1)} %raw_ref.4), channel_id=1, source_target_pairs={{0,124},{1,125},{2,126},{3,127},{4,0},{5,1},{6,2},{7,3},{8,4},{9,5... | collective-permute-start | bytes 7077896 | tf_op jit(solution)/shard_map/ppermute | solution.py:24
  6.7 31.2 %collective-permute-start.5 = (bf16[512,1152]{1,0:T(8,128)(2,1)}, bf16[512,1152]{1,0:T(8,128)(2,1)}, u32[]{:S(2)}, u32[]{:S(2)}) collective-permute-start(bf16[512,1152]{1,0:T(8,128)(2,1)} %get-tuple-element.30), channel_id=1, source_target_pairs={{0,1},{1,2},{2,3},{3,0},{4,5},{5,6},{6,7},{7,4},{8,9},{9,10},{10,1... | collective-permute-start | bytes 3538952 | tf_op jit(solution)/shard_map/ppermute | solution.py:24
  8.6 29.3 %collective-permute-start.3 = (bf16[512,1152]{1,0:T(8,128)(2,1)}, bf16[512,1152]{1,0:T(8,128)(2,1)}, u32[]{:S(2)}, u32[]{:S(2)}) collective-permute-start(bf16[512,1152]{1,0:T(8,128)(2,1)} %get-tuple-element.31), channel_id=1, source_target_pairs={{0,3},{1,0},{2,1},{3,2},{4,7},{5,4},{6,5},{7,6},{8,11},{9,8},{10,9... | collective-permute-start | bytes 3538952 | tf_op jit(solution)/shard_map/ppermute | solution.py:24
  10.7 102.4 %collective-permute-start.2 = (bf16[512,1152]{1,0:T(8,128)(2,1)}, bf16[512,1152]{1,0:T(8,128)(2,1)}, u32[]{:S(2)}, u32[]{:S(2)}) collective-permute-start(bf16[512,1152]{1,0:T(8,128)(2,1)} %get-tuple-element.30), channel_id=1, source_target_pairs={{0,3},{1,0},{2,1},{3,2},{4,7},{5,4},{6,5},{7,6},{8,11},{9,8},{10,9... | collective-permute-start | bytes 3538952 | tf_op jit(solution)/shard_map/ppermute | solution.py:24
  12.7 114.2 %collective-permute-start = (bf16[512,1152]{1,0:T(8,128)(2,1)}, bf16[512,1152]{1,0:T(8,128)(2,1)S(1)}, u32[]{:S(2)}, u32[]{:S(2)}) collective-permute-start(bf16[512,1152]{1,0:T(8,128)(2,1)} %get-tuple-element.31), channel_id=1, source_target_pairs={{0,1},{1,2},{2,3},{3,0},{4,5},{5,6},{6,7},{7,4},{8,9},{9,10},{10,1... | collective-permute-start | bytes 3538952 | tf_op jit(solution)/shard_map/ppermute | solution.py:24
  14.0 27.0 %copy-start = (bf16[1024,1152]{1,0:T(8,128)(2,1)S(1)}, bf16[1024,1152]{1,0:T(8,128)(2,1)}, u32[]{:S(2)}) copy-start(bf16[1024,1152]{1,0:T(8,128)(2,1)} %raw_ref.5) | copy-start | bytes 7077892
  37.9 50.5 %collective-permute-start.6 = (bf16[512,1152]{1,0:T(8,128)(2,1)}, bf16[512,1152]{1,0:T(8,128)(2,1)}, u32[]{:S(2)}, u32[]{:S(2)}) collective-permute-start(bf16[512,1152]{1,0:T(8,128)(2,1)} %collective-permute-done.5.text_ref), channel_id=1, source_target_pairs={{0,1},{1,2},{2,3},{3,0},{4,5},{5,6},{6,7},{7,4},{8,9},{9,10},{10,1... | collective-permute-start | bytes 3538952 | tf_op jit(solution)/shard_map/ppermute | solution.py:24
  37.9 61.2 %collective-permute-start.4 = (bf16[512,1152]{1,0:T(8,128)(2,1)}, bf16[512,1152]{1,0:T(8,128)(2,1)}, u32[]{:S(2)}, u32[]{:S(2)}) collective-permute-start(bf16[512,1152]{1,0:T(8,128)(2,1)} %collective-permute-done.3.text_ref), channel_id=1, source_target_pairs={{0,3},{1,0},{2,1},{3,2},{4,7},{5,4},{6,5},{7,6},{8,11},{9,8},{10,9... | collective-permute-start | bytes 3538952 | tf_op jit(solution)/shard_map/ppermute | solution.py:24
  98.9 41.9 %collective-permute-start.10 = (bf16[512,1152]{1,0:T(8,128)(2,1)S(1)}, bf16[512,1152]{1,0:T(8,128)(2,1)S(1)}, u32[]{:S(2)}, u32[]{:S(2)}) collective-permute-start(bf16[512,1152]{1,0:T(8,128)(2,1)S(1)} %get-tuple-element.27), channel_id=1, source_target_pairs={{0,1},{1,2},{2,3},{3,0},{4,5},{5,6},{6,7},{7,4},{8,9},{9,10},{10,1... | collective-permute-start | bytes 3538952 | tf_op jit(solution)/shard_map/ppermute | solution.py:24
  109.7 31.6 %collective-permute-start.12 = (bf16[512,1152]{1,0:T(8,128)(2,1)S(1)}, bf16[512,1152]{1,0:T(8,128)(2,1)}, u32[]{:S(2)}, u32[]{:S(2)}) collective-permute-start(bf16[512,1152]{1,0:T(8,128)(2,1)S(1)} %get-tuple-element.29), channel_id=1, source_target_pairs={{0,3},{1,0},{2,1},{3,2},{4,7},{5,4},{6,5},{7,6},{8,11},{9,8},{10,9... | collective-permute-start | bytes 3538952 | tf_op jit(solution)/shard_map/ppermute | solution.py:24
  113.1 41.2 %collective-permute-start.9 = (bf16[512,1152]{1,0:T(8,128)(2,1)S(1)}, bf16[512,1152]{1,0:T(8,128)(2,1)S(1)}, u32[]{:S(2)}, u32[]{:S(2)}) collective-permute-start(bf16[512,1152]{1,0:T(8,128)(2,1)S(1)} %get-tuple-element.25), channel_id=1, source_target_pairs={{0,1},{1,2},{2,3},{3,0},{4,5},{5,6},{6,7},{7,4},{8,9},{9,10},{10,1... | collective-permute-start | bytes 3538952 | tf_op jit(solution)/shard_map/ppermute | solution.py:24
  113.1 51.7 %collective-permute-start.8 = (bf16[512,1152]{1,0:T(8,128)(2,1)S(1)}, bf16[512,1152]{1,0:T(8,128)(2,1)S(1)}, u32[]{:S(2)}, u32[]{:S(2)}) collective-permute-start(bf16[512,1152]{1,0:T(8,128)(2,1)S(1)} %get-tuple-element.24), channel_id=1, source_target_pairs={{0,3},{1,0},{2,1},{3,2},{4,7},{5,4},{6,5},{7,6},{8,11},{9,8},{10,9... | collective-permute-start | bytes 3538952 | tf_op jit(solution)/shard_map/ppermute | solution.py:24
  140.8 58.7 %collective-permute-start.7 = (bf16[1024,1152]{1,0:T(8,128)(2,1)}, bf16[1024,1152]{1,0:T(8,128)(2,1)S(1)}, u32[]{:S(2)}, u32[]{:S(2)}) collective-permute-start(bf16[1024,1152]{1,0:T(8,128)(2,1)} %fusion), channel_id=1, source_target_pairs={{0,4},{1,5},{2,6},{3,7},{4,8},{5,9},{6,10},{7,11},{8,12},{9,13},{1... | collective-permute-start | bytes 7077896 | tf_op jit(solution)/shard_map/ppermute | solution.py:24
  141.1 37.5 %collective-permute-start.11 = (bf16[512,1152]{1,0:T(8,128)(2,1)S(1)}, bf16[512,1152]{1,0:T(8,128)(2,1)S(1)}, u32[]{:S(2)}, u32[]{:S(2)}) collective-permute-start(bf16[512,1152]{1,0:T(8,128)(2,1)S(1)} %add_convert_fusion.1), channel_id=1, source_target_pairs={{0,1},{1,2},{2,3},{3,0},{4,5},{5,6},{6,7},{7,4},{8,9},{9,10},{10,1... | collective-permute-start | bytes 3538952 | tf_op jit(solution)/shard_map/ppermute | solution.py:24
  142.8 46.0 %collective-permute-start.13 = (bf16[512,1152]{1,0:T(8,128)(2,1)S(1)}, bf16[512,1152]{1,0:T(8,128)(2,1)S(1)}, u32[]{:S(2)}, u32[]{:S(2)}) collective-permute-start(bf16[512,1152]{1,0:T(8,128)(2,1)S(1)} %add_convert_fusion), channel_id=1, source_target_pairs={{0,3},{1,0},{2,1},{3,2},{4,7},{5,4},{6,5},{7,6},{8,11},{9,8},{10,9... | collective-permute-start | bytes 3538952 | tf_op jit(solution)/shard_map/ppermute | solution.py:24
  199.5 1.4 copy-start.1
